TPU v7x, 32 devices: a whole 2x2x4 slice. The times are simulated.
32 devices in a mesh: case: 2 (over x), tile: 16 (over z, y, core).
Axes of the slice: x: 2, y: 2, z: 4, core: 2. Of those that a mesh axis runs over, the one named last changes fastest.
Arguments:
- node_coords: float32 [256, 3, 512], P(('case', 'tile')), parts along dimension 0, may hold values from 0 to 2.8
- node_sens: float32 [256, 3, 512], P(('case', 'tile')), parts along dimension 0, may hold values from -1.5 to 1.5
- centre_coords: float32 [3, 61440], P(None, ('case', 'tile')), parts along dimension 1, may hold values from 0 to 2.8
- centre_weights: float32 [3, 61440], P(None, ('case', 'tile')), parts along dimension 1, may hold values from -4 to 4
- pair_list: int32 [2, 8192], P(None, ('case', 'tile')), parts along dimension 1, may hold values from 0 to 239, as said below
- pair_count: int32 [32], P(('case', 'tile')), parts along dimension 0, may hold values from 1 to 256, as said below
Outputs:
- weight_grad: float32 [3, 61440], P(None, ('case', 'tile')), parts along dimension 1
- centre_grad: float32 [3, 61440], P(None, ('case', 'tile')), parts along dimension 1
There are 2 independent parts, one for each index of `case`. A program takes and returns all parts, laid end to end along the dimension named above; each array names one. Nothing has to cross between parts.
Inputs may be any that keep to these rules, and one draw needn't show every extreme that they name: `pair_list`: row 0 holds centre blocks; a slot of device d names only blocks b with d - 2 <= b // 15 <= d + 2. Row 1 holds tiles 0 to 7. `pair_count`: at most 256 live slots a device, reached on some device; at least 1.
All inputs are finite; a program needn't handle non-finite values.
Results may differ from a plain program's by a relative error of at most 0.0003.
Values sent between devices are 32-bit elements; how exact they have to be, the bound alone decides.
No kernel may reach another device: no remote copies, remote signals or barrier semaphores. Data moves between devices by JAX's collectives and lax.ppermute only.
A program may use at most 64 MiB of HBM per device.

v0:
```python
import functools

import jax
import jax.numpy as jnp
from jax import lax
from jax.experimental import pallas as pl
from jax.experimental.pallas import tpu as pltpu
from jax.sharding import PartitionSpec as P

CENTRE_BLOCK = 128
REACH = 2
MIDDLE = 1.4
SCALE = 8.0
TINY = 1e-30

F32 = jnp.float32
BF16 = jnp.bfloat16
F8 = jnp.float8_e4m3fn


def swap(array, axis, by, phase):
    devices = lax.axis_size(axis)
    pairs = []
    for i in range(devices - by):
        if (i // by) % 2 == phase:
            pairs += [(i, i + by), (i + by, i)]
    return lax.ppermute(array, axis, pairs)


def dot(a, b):
    return lax.dot_general(a, b, (((1,), (0,)), ((), ())), preferred_element_type=F32)


def split2(x):
    high = x.astype(BF16)
    return high, (x - high.astype(F32)).astype(BF16)


def split3(x):
    one = x.astype(BF16).astype(F32)
    rest = x - one
    two = rest.astype(BF16).astype(F32)
    return one, two, rest - two


def prepare_centres(centres, table_ref, block):
    a = (centres - MIDDLE) * (SCALE / 2)
    norm = jnp.sum(a * a, axis=0, keepdims=True)
    a1, a2, a3 = split3(a * -2.0)
    n1, n2, n3 = split3(norm)
    ones = jnp.ones((3, CENTRE_BLOCK), F32)
    pad = jnp.zeros((2, CENTRE_BLOCK), F32)
    rows = [a1, a2, a3, a1, a2, a1, ones, n1, n2, n3, a3, a2, pad]
    table_ref[block] = jnp.concatenate(rows, 0).astype(BF16)


def prepare_source(packed_ref, nodes_ref, sens_ref, small_ref, inverse_ref, rows_ref, source):
    place = [(packed_ref[j] - MIDDLE) * (SCALE / 2) for j in range(3)]
    sens = [packed_ref[3 + k] for k in range(3)]
    parts = [split3(x) for x in place]
    q1, q2, q3 = ([p[i] for p in parts] for i in range(3))
    norm = split3(place[0] * place[0] + place[1] * place[1] + place[2] * place[2])
    one = jnp.ones_like(place[0])
    zero = jnp.zeros_like(one)
    groups = one.shape[1] // 128
    kinds = q1 * 3 + q2 * 2 + q3 + list(norm) + [one] * 3 + q2 + q3 + [zero] * 2
    moments = sens + [s * place[j] for j in range(3) for s in sens]
    halves = [split2(m) for m in moments]
    high = [h.astype(F32) for h, _ in halves]
    low = [l.astype(F32) for _, l in halves]
    kinds += high[:3] + low[:3] + [zero] * 10 + high + low + [zero] * 8
    largest = functools.reduce(jnp.maximum, [jnp.abs(m) for m in moments])
    largest = jnp.maximum(jnp.max(largest, axis=(0, 1), keepdims=True), TINY)
    inverse_ref[source] = jnp.broadcast_to(largest * (1.0 / 128.0), (8, 128))
    small = [m * (128.0 / largest) for m in moments]
    upper = [m.astype(F8).astype(F32) for m in small]
    kinds += upper + [m - h for m, h in zip(small, upper)] + [zero] * 8
    for kind, value in enumerate(kinds):
        for g in range(groups):
            rows_ref[g, 8 * kind : 8 * kind + 8] = value[:, g * 128 : (g + 1) * 128]
    for t in range(8):
        for g in range(groups):
            lanes = slice(g * 128, (g + 1) * 128)
            rows = rows_ref[g, pl.ds(t, 32, stride=8), :].astype(BF16)
            nodes_ref[8 * source + t, lanes] = jnp.concatenate([rows, rows], 0).T
            sens_ref[8 * source + t, :, lanes] = rows_ref[g, pl.ds(256 + t, 48, stride=8), :].astype(BF16)
            small_ref[8 * source + t, :, lanes] = rows_ref[g, pl.ds(640 + t, 32, stride=8), :].astype(F8)


def list_pairs(codes, first, blocks, rows):
    slots = 8 * blocks
    lanes = CENTRE_BLOCK
    j_row = lax.broadcasted_iota(jnp.int32, (lanes, lanes), 0)
    j_col = lax.broadcasted_iota(jnp.int32, (lanes, lanes), 1)
    before = (j_col < j_row).astype(F32).astype(BF16)
    ones = jnp.ones((codes[0].shape[1], lanes), BF16)
    base = jnp.zeros((1, lanes), F32)
    listed = [jnp.zeros((1, lanes), F32)] * rows
    j_wide = lax.broadcasted_iota(jnp.int32, (lanes, codes[0].shape[1]), 0)
    for source, row in enumerate(codes):
        local = row.astype(jnp.int32) - 1 - 8 * first
        hit = ((local == j_wide) & (j_wide < slots)).astype(F32).astype(BF16)
        times = dot(hit, ones)
        active = times > 0.0
        flag = active.astype(F32)
        position = dot(before, flag.astype(BF16)) + base
        position = jnp.where(active, position, -1.0).astype(jnp.int32)
        value = (source * lanes + j_row).astype(F32) + 1024.0 * times
        for g in range(rows):
            here = jnp.where(position == j_col + g * lanes, value, 0.0)
            listed[g] = listed[g] + jnp.sum(here, axis=0, keepdims=True)
        base = base + jnp.sum(flag, axis=0, keepdims=True)
    fill = [jnp.zeros((1, lanes), F32)] * (7 - rows)
    return jnp.concatenate(listed + [base] + fill, 0).astype(jnp.int32)


def profile(s):
    s = jnp.minimum(jnp.maximum(s, TINY), SCALE * SCALE)
    r = s * lax.rsqrt(s)
    u = SCALE - r
    u2 = u * u
    u3 = u2 * u
    u4 = u2 * u2
    return u4 * (SCALE / 4 + r), u3


def split_small(x):
    high = x.astype(BF16)
    return high, (x - high.astype(F32)).astype(F8)


def run_pairs(list_ref, count, table_ref, tables, total_ref, work):
    nodes_ref, sens_ref, small_ref, inverse_ref = tables
    s0, s1, f0, f1, g0, g1 = work

    def item(k):
        value = list_ref[k // 128, k % 128]
        code = value % 1024
        tile = (code // 128) * 8 + code % 8
        block = (code % 128) // 8
        return tile, block, (value // 1024).astype(F32), code // 128

    def items(p):
        p = jnp.maximum(p, 0)
        return item(2 * p), item(2 * p + 1)

    lane = lax.broadcasted_iota(jnp.int32, (512, 64), 1)

    def distances(p, out):
        (t1, b1, _, _), (t2, b2, _, _) = items(p)
        zero = jnp.zeros((32, 128), BF16)
        rhs = jnp.concatenate(
            [jnp.concatenate([table_ref[b1], zero], 1), jnp.concatenate([zero, table_ref[b2]], 1)], 0
        )
        lhs = jnp.where(lane < 32, nodes_ref[t1], nodes_ref[t2])
        out[...] = dot(lhs, rhs)

    def profiles(s_ref, out, low):
        for k in range(0, 512, 64):
            rows = slice(k, k + 64)
            kernel, slope = profile(s_ref[rows])
            out[0, rows], low[0, rows] = split_small(kernel)
            out[1, rows], low[1, rows] = split_small(slope)

    def sums(p, f_ref, g_ref):
        (t1, b1, m1, o1), (t2, b2, m2, o2) = items(p)
        left, right = sens_ref[t1], sens_ref[t2]
        kernel = dot(jnp.concatenate([left[0:16], right[0:16]], 0), f_ref[0])
        small = jnp.concatenate([small_ref[t1], small_ref[t2]], 0)
        kernel_low = dot(small, g_ref[0])
        slope = dot(jnp.concatenate([left[16:48], right[16:48]], 0), f_ref[1])
        slope_low = dot(small, g_ref[1])
        w1 = (m1 * inverse_ref[o1])[0:1]
        w2 = (m2 * inverse_ref[o2])[0:1]
        total_ref[b1, 0:8] += m1 * kernel[0:8, :128]
        total_ref[b1, 8:32] += m1 * slope[0:24, :128]
        total_ref[b1, 32:48] += w1 * kernel_low[0:16, :128]
        total_ref[b1, 48:72] += w1 * slope_low[0:24, :128]
        total_ref[b2, 0:8] += m2 * kernel[16:24, 128:]
        total_ref[b2, 8:32] += m2 * slope[32:56, 128:]
        total_ref[b2, 32:48] += w2 * kernel_low[32:48, 128:]
        total_ref[b2, 48:72] += w2 * slope_low[32:56, 128:]

    units = (count + 3) // 4

    @pl.when(units > 0)
    def _():
        distances(0, s0)
        f1[...] = jnp.zeros_like(f1)
        g1[...] = jnp.zeros_like(g1)

        def unit(j):
            p = 2 * j
            sums(p - 1, f1, g1)
            distances(p + 1, s1)
            profiles(s0, f0, g0)
            sums(p, f0, g0)
            distances(p + 2, s0)
            profiles(s1, f1, g1)

        def long_step(j, carry):
            for k in range(4):
                unit(4 * j + k)
            return carry

        def short_step(j, carry):
            unit(j)
            return carry

        lax.fori_loop(0, units // 4, long_step, 0)
        lax.fori_loop(units // 4 * 4, units, short_step, 0)
        sums(2 * units - 1, f1, g1)


def own_kernel(packed_ref, centres_ref, first_ref, total_ref, table_ref, *scratch):
    *tables, rows_ref, list_vmem, list_smem, sem = scratch[:8]
    work = scratch[8:]
    blocks = table_ref.shape[0]
    for block in range(blocks):
        prepare_centres(centres_ref[:, block * 128 : (block + 1) * 128], table_ref, block)
    list_vmem[...] = list_pairs([packed_ref[6, 0:1, 0:256]], first_ref[0], blocks, 2)
    copy = pltpu.make_async_copy(list_vmem, list_smem, sem)
    copy.start()
    total_ref[...] = jnp.zeros_like(total_ref)
    prepare_source(packed_ref, *tables, rows_ref.at[0], 0)
    copy.wait()
    run_pairs(list_smem, list_smem[2, 0], table_ref, tables, total_ref, work)


def near_kernel(p0, p1, p2, p3, centres_ref, weights_ref, first_ref, before_ref, table_ref, *rest):
    grad_w, grad_c, total_ref, *tables = rest[:7]
    rows_ref, list_vmem, list_smem, sem = rest[7:11]
    work = rest[11:]
    packed = (p0, p1, p2, p3)
    blocks = table_ref.shape[0]
    list_vmem[...] = list_pairs([p[6, 0:1, 0:256] for p in packed], first_ref[0], blocks, 5)
    copy = pltpu.make_async_copy(list_vmem, list_smem, sem)
    copy.start()
    total_ref[...] = before_ref[...]
    for source, ref in enumerate(packed):
        prepare_source(ref, *tables, rows_ref.at[source], source)
    copy.wait()
    run_pairs(list_smem, list_smem[5, 0], table_ref, tables, total_ref, work)
    for block in range(blocks):
        total = total_ref[block]
        here = slice(block * 128, (block + 1) * 128)
        grad_w[:, here] = (4.0 / SCALE**5) * (total[0:3] + total[3:6] + (total[32:35] + total[44:47]))
        both = total[8:20] + total[20:32] + (total[48:60] + total[60:72])
        a = (centres_ref[:, here] - MIDDLE) * (SCALE / 2)
        w = weights_ref[:, here] * (-10.0 / SCALE**4)
        for j in range(3):
            terms = w * (a[j : j + 1] * both[0:3] - both[3 + 3 * j : 6 + 3 * j])
            grad_c[j : j + 1, here] = jnp.sum(terms, axis=0, keepdims=True)


def body(node_coords, node_sens, centre_coords, centre_weights, pair_list, pair_count):
    device = lax.axis_index("tile")
    tiles, _, nodes = node_coords.shape
    slots = pair_list.shape[1]
    blocks = centre_coords.shape[1] // CENTRE_BLOCK
    code = pair_list[0] * 8 + pair_list[1] + 1
    code = jnp.where(jnp.arange(slots) < pair_count[0], code, 0).astype(F32)
    code = jnp.pad(code[None, None], ((0, 0), (0, tiles - 1), (0, nodes - slots)))
    packed = jnp.concatenate([node_coords.transpose(1, 0, 2), node_sens.transpose(1, 0, 2), code], 0)
    near = [swap(packed, "tile", by, phase) for by in (1, 2) for phase in (0, 1)]
    first = (device * blocks).astype(jnp.int32).reshape(1)

    vmem = pl.BlockSpec(memory_space=pltpu.VMEM)
    smem = pl.BlockSpec(memory_space=pltpu.SMEM)

    def scratch(count):
        return [
            pltpu.VMEM((count, nodes, 64), BF16),
            pltpu.VMEM((count, 48, nodes), BF16),
            pltpu.VMEM((count, 32, nodes), F8),
            pltpu.VMEM((count // 8, 8, 128), F32),
            pltpu.VMEM((count // 8, nodes // 128, 112 * 8, 128), F32),
            pltpu.VMEM((8, 128), jnp.int32),
            pltpu.SMEM((8, 128), jnp.int32),
            pltpu.SemaphoreType.DMA,
            pltpu.VMEM((nodes, 256), F32),
            pltpu.VMEM((nodes, 256), F32),
            pltpu.VMEM((2, nodes, 256), BF16),
            pltpu.VMEM((2, nodes, 256), BF16),
            pltpu.VMEM((2, nodes, 256), F8),
            pltpu.VMEM((2, nodes, 256), F8),
        ]

    params = pltpu.CompilerParams(vmem_limit_bytes=40 << 20)
    total_type = jax.ShapeDtypeStruct((blocks, 72, 128), F32)
    own, table = pl.pallas_call(
        own_kernel,
        out_shape=(total_type, jax.ShapeDtypeStruct((blocks, 32, 128), BF16)),
        in_specs=[vmem, vmem, smem],
        out_specs=(vmem, vmem),
        scratch_shapes=scratch(tiles),
        compiler_params=params,
        cost_estimate=pl.CostEstimate(flops=10**9, bytes_accessed=10**6, transcendentals=0),
        name="own_pairs",
    )(packed, centre_coords, first)
    grads = jax.ShapeDtypeStruct(centre_coords.shape, F32)
    return pl.pallas_call(
        near_kernel,
        out_shape=(grads, grads),
        in_specs=[vmem] * 6 + [smem] + [vmem] * 2,
        out_specs=(vmem, vmem),
        scratch_shapes=[pltpu.VMEM((blocks, 72, 128), F32)] + scratch(4 * tiles),
        compiler_params=params,
        name="near_pairs",
    )(*near, centre_coords, centre_weights, first, own, table)


def solution(mesh):
    return jax.shard_map(
        body,
        mesh=mesh,
        in_specs=(
            P(("case", "tile"), None, None),
            P(("case", "tile"), None, None),
            P(None, ("case", "tile")),
            P(None, ("case", "tile")),
            P(None, ("case", "tile")),
            P(("case", "tile")),
        ),
        out_specs=(P(None, ("case", "tile")), P(None, ("case", "tile"))),
        check_vma=False,
    )
```

profile of v0, /device:TPU:7, one launch (start us, length us, event | category | flops | bytes accessed | tf_op | source)
XLA Modules:
  0.0 53.0 jit_solution(1196134898754639660)
XLA Ops:
  0.6 0.0 copy-start.2
  1.3 0.0 copy-done.2
  1.3 0.0 copy-start
  1.3 0.8 %select_maximum_fusion.packed_ref = f32[7,8,512]{2,1,0:T(8,128)S(1)} fusion(f32[1,1,256]{2,1,0:T(1,128)S(1)} %fusion, f32[3,8,512]{2,1,0:T(8,128)} %bitcast.7, f32[3,8,512]{2,1,0:T(8,128)} %bitcast.8), kind=kLoop, calls=%fused_computation | loop fusion | flops 114688 | bytes 214016 | tf_op jit(solution)/shard_map/concatenate | solution.py:264
  2.2 3.1 %collective-permute-start.3 = (f32[7,8,512]{2,1,0:T(8,128)S(1)}, f32[7,8,512]{2,1,0:T(8,128)S(1)}, u32[]{:S(2)}, u32[]{:S(2)}) collective-permute-start(f32[7,8,512]{2,1,0:T(8,128)S(1)} %select_maximum_fusion.packed_ref), channel_id=1, source_target_pairs={{2,4},{4,2},{3,5},{5,3},{6,8},{8,6},{7,9},{9,7},{10,12},{12,10},{1... | collective-permute-start | bytes 344072 | tf_op jit(solution)/shard_map/ppermute | solution.py:27
  5.3 0.1 collective-permute-start.2
  5.4 5.5 %collective-permute-start.1 = (f32[7,8,512]{2,1,0:T(8,128)S(1)}, f32[7,8,512]{2,1,0:T(8,128)S(1)}, u32[]{:S(2)}, u32[]{:S(2)}) collective-permute-start(f32[7,8,512]{2,1,0:T(8,128)S(1)} %select_maximum_fusion.packed_ref), channel_id=1, source_target_pairs={{1,2},{2,1},{3,4},{4,3},{5,6},{6,5},{7,8},{8,7},{9,10},{10,9},{11,... | collective-permute-start | bytes 344072 | tf_op jit(solution)/shard_map/ppermute | solution.py:27
  10.9 0.1 collective-permute-start
  11.0 0.0 copy-done
  11.0 0.0 copy-start.1
  11.0 9.4 %own_pairs.1 = (f32[15,72,128]{2,1,0:T(8,128)S(1)}, bf16[15,32,128]{2,1,0:T(8,128)(2,1)S(1)}) custom-call(f32[7,8,512]{2,1,0:T(8,128)S(1)} %select_maximum_fusion.packed_ref, f32[3,1920]{1,0:T(4,128)S(1)} %copy-done, s32[1]{0:T(128)} %bitcast.4.first_ref), custom_call_target="tpu_custom_call" | custom-call | flops 1000000000 | bytes 1000000 | tf_op jit(solution)/shard_map/own_pairs/pallas_call | solution.py:291
  20.4 0.0 collective-permute-done.3.p3
  20.4 0.0 collective-permute-done.2.p2
  20.4 0.0 collective-permute-done.1.p1
  20.5 0.0 collective-permute-done.p0
  20.5 0.0 copy-done.1
  20.5 32.5 %near_pairs.1 = (f32[3,1920]{1,0:T(4,128)}, f32[3,1920]{1,0:T(4,128)}) custom-call(f32[7,8,512]{2,1,0:T(8,128)S(1)} %collective-permute-done.p0, f32[7,8,512]{2,1,0:T(8,128)S(1)} %collective-permute-done.1.p1, f32[7,8,512]{2,1,0:T(8,128)S(1)} %collective-permute-done.2.p2, f32[7,8,512]{2,1,0:T(8,128)S(1)} %collective-permute-done.3.p3, ...), custom_call_target="tpu_custom_call" | custom-call | tf_op jit(solution)/shard_map/near_pairs/pallas_call | solution.py:302
  (1 shorter events, 0.0 us)
Async XLA Ops:
  0.6 0.7 %copy-start.2 = (s32[2,256]{1,0:T(2,128)S(1)}, s32[2,256]{1,0:T(2,128)}, u32[]{:S(2)}) copy-start(s32[2,256]{1,0:T(2,128)} %param.10) | copy-start | bytes 6148
  1.3 9.7 %copy-start = (f32[3,1920]{1,0:T(4,128)S(1)}, f32[3,1920]{1,0:T(4,128)}, u32[]{:S(2)}) copy-start(f32[3,1920]{1,0:T(4,128)} %centres_ref.3) | copy-start | bytes 69124
  2.2 18.3 %collective-permute-start.3 = (f32[7,8,512]{2,1,0:T(8,128)S(1)}, f32[7,8,512]{2,1,0:T(8,128)S(1)}, u32[]{:S(2)}, u32[]{:S(2)}) collective-permute-start(f32[7,8,512]{2,1,0:T(8,128)S(1)} %select_maximum_fusion.packed_ref), channel_id=1, source_target_pairs={{2,4},{4,2},{3,5},{5,3},{6,8},{8,6},{7,9},{9,7},{10,12},{12,10},{1... | collective-permute-start | bytes 344072 | tf_op jit(solution)/shard_map/ppermute | solution.py:27
  5.3 15.1 %collective-permute-start.2 = (f32[7,8,512]{2,1,0:T(8,128)S(1)}, f32[7,8,512]{2,1,0:T(8,128)S(1)}, u32[]{:S(2)}, u32[]{:S(2)}) collective-permute-start(f32[7,8,512]{2,1,0:T(8,128)S(1)} %select_maximum_fusion.packed_ref), channel_id=1, source_target_pairs={{0,2},{2,0},{1,3},{3,1},{4,6},{6,4},{5,7},{7,5},{8,10},{10,8},{9,1... | collective-permute-start | bytes 344072 | tf_op jit(solution)/shard_map/ppermute | solution.py:27
  5.4 15.0 %collective-permute-start.1 = (f32[7,8,512]{2,1,0:T(8,128)S(1)}, f32[7,8,512]{2,1,0:T(8,128)S(1)}, u32[]{:S(2)}, u32[]{:S(2)}) collective-permute-start(f32[7,8,512]{2,1,0:T(8,128)S(1)} %select_maximum_fusion.packed_ref), channel_id=1, source_target_pairs={{1,2},{2,1},{3,4},{4,3},{5,6},{6,5},{7,8},{8,7},{9,10},{10,9},{11,... | collective-permute-start | bytes 344072 | tf_op jit(solution)/shard_map/ppermute | solution.py:27
  10.9 9.6 %collective-permute-start = (f32[7,8,512]{2,1,0:T(8,128)S(1)}, f32[7,8,512]{2,1,0:T(8,128)S(1)}, u32[]{:S(2)}, u32[]{:S(2)}) collective-permute-start(f32[7,8,512]{2,1,0:T(8,128)S(1)} %select_maximum_fusion.packed_ref), channel_id=1, source_target_pairs={{0,1},{1,0},{2,3},{3,2},{4,5},{5,4},{6,7},{7,6},{8,9},{9,8},{10,11... | collective-permute-start | bytes 344072 | tf_op jit(solution)/shard_map/ppermute | solution.py:27
  11.0 9.5 %copy-start.1 = (f32[3,1920]{1,0:T(4,128)S(1)}, f32[3,1920]{1,0:T(4,128)}, u32[]{:S(2)}) copy-start(f32[3,1920]{1,0:T(4,128)} %weights_ref.1) | copy-start | bytes 69124
where the time goes:
time: 52.5 us; the launch traced here: 53 us
  Pallas kernels  41.9 us (80%)
  starting transfers between devices  8.77 us (17%)
  between operations  1.41 us (3%)
  other arithmetic  0.84 us (2%)
    pallas_call x1, Pallas kernels, body(): pl.pallas_call(near_kernel, out_shape=(grads, grads), in_specs=[vmem] * 6...  32.5 us
    pallas_call x1, Pallas kernels, body(): pl.pallas_call(own_kernel, out_shape=(total_type, jax.ShapeDtypeStruct((b...  9.42 us
    ppermute x4, starting transfers between devices, swap(): return lax.ppermute(array, axis, pairs)  8.77 us
  transfers between devices with their start and end apart: 4, of which 0 were waited for; matrix products, arithmetic and copies ran while one was open for 0% of the time, Pallas kernels for 18%

commit v1 on v0

--- a/solution.py
+++ b/solution.py
@@ -49,8 +49,8 @@
     a1, a2, a3 = split3(a * -2.0)
     n1, n2, n3 = split3(norm)
     ones = jnp.ones((3, CENTRE_BLOCK), F32)
-    pad = jnp.zeros((2, CENTRE_BLOCK), F32)
-    rows = [a1, a2, a3, a1, a2, a1, ones, n1, n2, n3, a3, a2, pad]
+    zeros = jnp.zeros((2, CENTRE_BLOCK), F32)
+    rows = [a1, a1, ones[:2], a2, a2, zeros, a3, a3, zeros, a1, ones[:1], n1, n2, n3, zeros[:1]]
     table_ref[block] = jnp.concatenate(rows, 0).astype(BF16)
 
 
@@ -63,28 +63,33 @@
     one = jnp.ones_like(place[0])
     zero = jnp.zeros_like(one)
     groups = one.shape[1] // 128
-    kinds = q1 * 3 + q2 * 2 + q3 + list(norm) + [one] * 3 + q2 + q3 + [zero] * 2
+    empty = jnp.zeros((8, 128), F32)
+    kinds = q1 + q2 + list(norm[:2]) + q3 + [norm[2], one, one, one, zero]
     moments = sens + [s * place[j] for j in range(3) for s in sens]
     halves = [split2(m) for m in moments]
     high = [h.astype(F32) for h, _ in halves]
     low = [l.astype(F32) for _, l in halves]
-    kinds += high[:3] + low[:3] + [zero] * 10 + high + low + [zero] * 8
+    kinds += high[:3] + low[:3] + high[3:] + low[3:]
     largest = functools.reduce(jnp.maximum, [jnp.abs(m) for m in moments])
     largest = jnp.maximum(jnp.max(largest, axis=(0, 1), keepdims=True), TINY)
     inverse_ref[source] = jnp.broadcast_to(largest * (1.0 / 128.0), (8, 128))
     small = [m * (128.0 / largest) for m in moments]
     upper = [m.astype(F8).astype(F32) for m in small]
-    kinds += upper + [m - h for m, h in zip(small, upper)] + [zero] * 8
+    kinds += upper + [m - h for m, h in zip(small, upper)]
     for kind, value in enumerate(kinds):
         for g in range(groups):
             rows_ref[g, 8 * kind : 8 * kind + 8] = value[:, g * 128 : (g + 1) * 128]
     for t in range(8):
         for g in range(groups):
             lanes = slice(g * 128, (g + 1) * 128)
-            rows = rows_ref[g, pl.ds(t, 32, stride=8), :].astype(BF16)
+            rows = rows_ref[g, pl.ds(t, 16, stride=8), :]
+            first, second = rows[0:8], rows[8:16]
+            rows = jnp.concatenate([first, first, first, second], 0).astype(BF16)
             nodes_ref[8 * source + t, lanes] = jnp.concatenate([rows, rows], 0).T
-            sens_ref[8 * source + t, :, lanes] = rows_ref[g, pl.ds(256 + t, 48, stride=8), :].astype(BF16)
-            small_ref[8 * source + t, :, lanes] = rows_ref[g, pl.ds(640 + t, 32, stride=8), :].astype(F8)
+            rows = jnp.concatenate([rows_ref[g, pl.ds(128 + t, 24, stride=8), :], empty], 0)
+            sens_ref[8 * source + t, :, lanes] = rows.astype(BF16)
+            rows = jnp.concatenate([rows_ref[g, pl.ds(320 + t, 24, stride=8), :], empty], 0)
+            small_ref[8 * source + t, :, lanes] = rows.astype(F8)
 
 
 def list_pairs(codes, first, blocks, rows):
@@ -116,7 +121,7 @@
 
 def profile(s):
     s = jnp.minimum(jnp.maximum(s, TINY), SCALE * SCALE)
-    r = s * lax.rsqrt(s)
+    r = pl.reciprocal(lax.rsqrt(s), approx=True)
     u = SCALE - r
     u2 = u * u
     u3 = u2 * u
@@ -168,7 +173,7 @@
         kernel = dot(jnp.concatenate([left[0:16], right[0:16]], 0), f_ref[0])
         small = jnp.concatenate([small_ref[t1], small_ref[t2]], 0)
         kernel_low = dot(small, g_ref[0])
-        slope = dot(jnp.concatenate([left[16:48], right[16:48]], 0), f_ref[1])
+        slope = dot(jnp.concatenate([left, right], 0), f_ref[1])
         slope_low = dot(small, g_ref[1])
         w1 = (m1 * inverse_ref[o1])[0:1]
         w2 = (m2 * inverse_ref[o2])[0:1]
@@ -245,11 +250,13 @@
         total = total_ref[block]
         here = slice(block * 128, (block + 1) * 128)
         grad_w[:, here] = (4.0 / SCALE**5) * (total[0:3] + total[3:6] + (total[32:35] + total[44:47]))
-        both = total[8:20] + total[20:32] + (total[48:60] + total[60:72])
+        low = total[48:60] + total[60:72]
+        plain = total[8:11] + total[11:14] + low[0:3]
+        moments = total[14:23] + total[23:32] + low[3:12]
         a = (centres_ref[:, here] - MIDDLE) * (SCALE / 2)
         w = weights_ref[:, here] * (-10.0 / SCALE**4)
         for j in range(3):
-            terms = w * (a[j : j + 1] * both[0:3] - both[3 + 3 * j : 6 + 3 * j])
+            terms = w * (a[j : j + 1] * plain - moments[3 * j : 3 * j + 3])
             grad_c[j : j + 1, here] = jnp.sum(terms, axis=0, keepdims=True)
 
 
@@ -271,10 +278,10 @@
     def scratch(count):
         return [
             pltpu.VMEM((count, nodes, 64), BF16),
-            pltpu.VMEM((count, 48, nodes), BF16),
+            pltpu.VMEM((count, 32, nodes), BF16),
             pltpu.VMEM((count, 32, nodes), F8),
             pltpu.VMEM((count // 8, 8, 128), F32),
-            pltpu.VMEM((count // 8, nodes // 128, 112 * 8, 128), F32),
+            pltpu.VMEM((count // 8, nodes // 128, 64 * 8, 128), F32),
             pltpu.VMEM((8, 128), jnp.int32),
             pltpu.SMEM((8, 128), jnp.int32),
             pltpu.SemaphoreType.DMA,

time: 52.5 us -> 48.3 us (0.920)
  the two profiles are of different devices: /device:TPU:7 before, /device:TPU:6 now
where the time goes in v1:
time: 48.3 us; the launch traced here: 47.3 us
  Pallas kernels  36.5 us (76%)
  starting transfers between devices  8.6 us (18%)
  between operations  1.38 us (3%)
  other arithmetic  0.84 us (2%)
    pallas_call x1, Pallas kernels, body(): pl.pallas_call(near_kernel, out_shape=(grads, grads), in_specs=[vmem] * 6...  29 us
    ppermute x4, starting transfers between devices, swap(): return lax.ppermute(array, axis, pairs)  8.6 us
    pallas_call x1, Pallas kernels, body(): pl.pallas_call(own_kernel, out_shape=(total_type, jax.ShapeDtypeStruct((b...  7.48 us
  transfers between devices with their start and end apart: 4, of which 0 were waited for; matrix products, arithmetic and copies ran while one was open for 0% of the time, Pallas kernels for 16%

profile of v1, /device:TPU:6, one launch (start us, length us, event | category | flops | bytes accessed | tf_op | source)
XLA Modules:
  0.0 47.3 jit_solution(110567008269277081)
XLA Ops:
  0.6 0.0 copy-start.2
  1.3 0.0 copy-done.2
  1.3 0.0 copy-start
  1.3 0.8 %select_maximum_fusion.packed_ref = f32[7,8,512]{2,1,0:T(8,128)S(1)} fusion(f32[1,1,256]{2,1,0:T(1,128)S(1)} %fusion, f32[3,8,512]{2,1,0:T(8,128)} %bitcast.7, f32[3,8,512]{2,1,0:T(8,128)} %bitcast.8), kind=kLoop, calls=%fused_computation | loop fusion | flops 114688 | bytes 214016 | tf_op jit(solution)/shard_map/concatenate | solution.py:271
  2.2 3.4 %collective-permute-start.3 = (f32[7,8,512]{2,1,0:T(8,128)S(1)}, f32[7,8,512]{2,1,0:T(8,128)S(1)}, u32[]{:S(2)}, u32[]{:S(2)}) collective-permute-start(f32[7,8,512]{2,1,0:T(8,128)S(1)} %select_maximum_fusion.packed_ref), channel_id=1, source_target_pairs={{2,4},{4,2},{3,5},{5,3},{6,8},{8,6},{7,9},{9,7},{10,12},{12,10},{1... | collective-permute-start | bytes 344072 | tf_op jit(solution)/shard_map/ppermute | solution.py:27
  5.6 0.1 collective-permute-start.2
  5.7 2.8 %collective-permute-start.1 = (f32[7,8,512]{2,1,0:T(8,128)S(1)}, f32[7,8,512]{2,1,0:T(8,128)S(1)}, u32[]{:S(2)}, u32[]{:S(2)}) collective-permute-start(f32[7,8,512]{2,1,0:T(8,128)S(1)} %select_maximum_fusion.packed_ref), channel_id=1, source_target_pairs={{1,2},{2,1},{3,4},{4,3},{5,6},{6,5},{7,8},{8,7},{9,10},{10,9},{11,... | collective-permute-start | bytes 344072 | tf_op jit(solution)/shard_map/ppermute | solution.py:27
  8.5 2.3 %collective-permute-start = (f32[7,8,512]{2,1,0:T(8,128)S(1)}, f32[7,8,512]{2,1,0:T(8,128)S(1)}, u32[]{:S(2)}, u32[]{:S(2)}) collective-permute-start(f32[7,8,512]{2,1,0:T(8,128)S(1)} %select_maximum_fusion.packed_ref), channel_id=1, source_target_pairs={{0,1},{1,0},{2,3},{3,2},{4,5},{5,4},{6,7},{7,6},{8,9},{9,8},{10,11... | collective-permute-start | bytes 344072 | tf_op jit(solution)/shard_map/ppermute | solution.py:27
  10.8 0.0 copy-done
  10.8 0.0 copy-start.1
  10.8 7.5 %own_pairs.1 = (f32[15,72,128]{2,1,0:T(8,128)S(1)}, bf16[15,32,128]{2,1,0:T(8,128)(2,1)S(1)}) custom-call(f32[7,8,512]{2,1,0:T(8,128)S(1)} %select_maximum_fusion.packed_ref, f32[3,1920]{1,0:T(4,128)S(1)} %copy-done, s32[1]{0:T(128)} %bitcast.4.first_ref), custom_call_target="tpu_custom_call" | custom-call | flops 1000000000 | bytes 1000000 | tf_op jit(solution)/shard_map/own_pairs/pallas_call | solution.py:298
  18.3 0.0 collective-permute-done.3.p3
  18.3 0.0 collective-permute-done.2.p2
  18.3 0.0 collective-permute-done.1.p1
  18.3 0.0 collective-permute-done.p0
  18.3 0.0 copy-done.1
  18.3 29.0 %near_pairs.1 = (f32[3,1920]{1,0:T(4,128)}, f32[3,1920]{1,0:T(4,128)}) custom-call(f32[7,8,512]{2,1,0:T(8,128)S(1)} %collective-permute-done.p0, f32[7,8,512]{2,1,0:T(8,128)S(1)} %collective-permute-done.1.p1, f32[7,8,512]{2,1,0:T(8,128)S(1)} %collective-permute-done.2.p2, f32[7,8,512]{2,1,0:T(8,128)S(1)} %collective-permute-done.3.p3, ...), custom_call_target="tpu_custom_call" | custom-call | tf_op jit(solution)/shard_map/near_pairs/pallas_call | solution.py:309
  (1 shorter events, 0.0 us)
Async XLA Ops:
  0.6 0.7 %copy-start.2 = (s32[2,256]{1,0:T(2,128)S(1)}, s32[2,256]{1,0:T(2,128)}, u32[]{:S(2)}) copy-start(s32[2,256]{1,0:T(2,128)} %param.10) | copy-start | bytes 6148
  1.3 9.5 %copy-start = (f32[3,1920]{1,0:T(4,128)S(1)}, f32[3,1920]{1,0:T(4,128)}, u32[]{:S(2)}) copy-start(f32[3,1920]{1,0:T(4,128)} %centres_ref.3) | copy-start | bytes 69124
  2.2 16.1 %collective-permute-start.3 = (f32[7,8,512]{2,1,0:T(8,128)S(1)}, f32[7,8,512]{2,1,0:T(8,128)S(1)}, u32[]{:S(2)}, u32[]{:S(2)}) collective-permute-start(f32[7,8,512]{2,1,0:T(8,128)S(1)} %select_maximum_fusion.packed_ref), channel_id=1, source_target_pairs={{2,4},{4,2},{3,5},{5,3},{6,8},{8,6},{7,9},{9,7},{10,12},{12,10},{1... | collective-permute-start | bytes 344072 | tf_op jit(solution)/shard_map/ppermute | solution.py:27
  5.6 12.7 %collective-permute-start.2 = (f32[7,8,512]{2,1,0:T(8,128)S(1)}, f32[7,8,512]{2,1,0:T(8,128)S(1)}, u32[]{:S(2)}, u32[]{:S(2)}) collective-permute-start(f32[7,8,512]{2,1,0:T(8,128)S(1)} %select_maximum_fusion.packed_ref), channel_id=1, source_target_pairs={{0,2},{2,0},{1,3},{3,1},{4,6},{6,4},{5,7},{7,5},{8,10},{10,8},{9,1... | collective-permute-start | bytes 344072 | tf_op jit(solution)/shard_map/ppermute | solution.py:27
  5.7 12.6 %collective-permute-start.1 = (f32[7,8,512]{2,1,0:T(8,128)S(1)}, f32[7,8,512]{2,1,0:T(8,128)S(1)}, u32[]{:S(2)}, u32[]{:S(2)}) collective-permute-start(f32[7,8,512]{2,1,0:T(8,128)S(1)} %select_maximum_fusion.packed_ref), channel_id=1, source_target_pairs={{1,2},{2,1},{3,4},{4,3},{5,6},{6,5},{7,8},{8,7},{9,10},{10,9},{11,... | collective-permute-start | bytes 344072 | tf_op jit(solution)/shard_map/ppermute | solution.py:27
  8.5 9.8 %collective-permute-start = (f32[7,8,512]{2,1,0:T(8,128)S(1)}, f32[7,8,512]{2,1,0:T(8,128)S(1)}, u32[]{:S(2)}, u32[]{:S(2)}) collective-permute-start(f32[7,8,512]{2,1,0:T(8,128)S(1)} %select_maximum_fusion.packed_ref), channel_id=1, source_target_pairs={{0,1},{1,0},{2,3},{3,2},{4,5},{5,4},{6,7},{7,6},{8,9},{9,8},{10,11... | collective-permute-start | bytes 344072 | tf_op jit(solution)/shard_map/ppermute | solution.py:27
  10.8 7.5 %copy-start.1 = (f32[3,1920]{1,0:T(4,128)S(1)}, f32[3,1920]{1,0:T(4,128)}, u32[]{:S(2)}) copy-start(f32[3,1920]{1,0:T(4,128)} %weights_ref.1) | copy-start | bytes 69124
